TPU v7x, 32 devices: a whole 2x2x4 slice. The times are simulated.
32 devices in a mesh: gx: 8 (over y, x, core), ga: 4 (over z).
Axes of the slice: x: 2, y: 2, z: 4, core: 2. Of those that a mesh axis runs over, the one named last changes fastest.
Arguments:
- velocity: float32 [3, 32, 384, 768], P(None, 'gx', 'ga'), may hold values from -6 to 6
- accumulated: float32 [3, 32, 384, 768], P(None, 'gx', 'ga'), may hold values from -6 to 6
- wall_first: float32 [384, 384], replicated, may hold values from -0.3125 to 0.3125
- wall_second: float32 [384, 384], replicated, may hold values from -0.3125 to 0.3125
- recycle_rows: int32 [384], replicated, may hold values from 0 to 382
- weight_index: int32 [384], replicated, may hold values from 0 to 63
- weight_table: float32 [64], replicated, may hold values from 0 to 1
Outputs:
- velocity_next: float32 [3, 32, 384, 768], P(None, 'gx', 'ga')
- accumulated_next: float32 [3, 32, 384, 768], P(None, 'gx', 'ga')
Inputs may be any that keep to these rules, and one draw needn't show every extreme that they name: `recycle_rows`: each entry names the lower of two adjacent recycle-plane rows. `weight_index`: each entry names one entry of weight_table.
All inputs are finite; a program needn't handle non-finite values.
Results may differ from a plain program's by a relative error of at most 0.0001.
Values sent between devices are 32-bit elements; how exact they have to be, the bound alone decides.
A program may use at most 128 MiB of HBM per device.

v0:
```python
import math

import jax
import jax.numpy as jnp
from jax import lax
from jax.sharding import PartitionSpec as P

HALO = 4


first_coef = (0.8, -0.2, 4.0 / 105.0, -1.0 / 280.0)
second_coef = (1.6, -0.2, 8.0 / 315.0, -1.0 / 560.0)
center_coef = -205.0 / 72.0
step_size = 0.2
viscosity = 0.2
keep_rate = -5.0 / 9.0
update_rate = 15.0 / 16.0


def padded_2(cells, sides, width):
    for axis, dim in sides:
        count = lax.axis_size(axis)
        ends = count - 1
        head = lax.slice_in_dim(cells, 0, width, axis=dim)
        tail = lax.slice_in_dim(cells, cells.shape[dim] - width, cells.shape[dim], axis=dim)
        cells = jnp.concatenate(
            [
                lax.ppermute(tail, axis, [(i, (i + 1) % count) for i in range(ends)]),
                cells,
                lax.ppermute(head, axis, [((i + 1) % count, i) for i in range(ends)]),
            ],
            axis=dim,
        )
    return cells


def passed_along(shard, axis, by):
    peers = lax.axis_size(axis)
    pairs = [(i, i + by) for i in range(peers) if 0 <= i + by < peers]
    return lax.ppermute(shard, axis, pairs)


def spanwise_table(length):
    places = jnp.arange(length, dtype=jnp.int32)
    apart = places[None, :] - places[:, None]
    apart = jnp.remainder(apart + length // 2, length) - length // 2
    parity = 1.0 - 2.0 * jnp.remainder(apart, 2).astype(jnp.float32)
    spacing = 2.0 * math.pi / length
    angle = apart.astype(jnp.float32) * (0.5 * spacing)
    same = apart == 0
    safe_sine = jnp.where(same, 1.0, jnp.sin(angle))
    first = jnp.where(same, 0.0, 0.5 * spacing * parity * jnp.cos(angle) / safe_sine)
    second = jnp.where(
        same,
        -math.pi * math.pi / 3.0 - spacing * spacing / 6.0,
        -0.5 * spacing * spacing * parity / (safe_sine * safe_sine),
    )
    return jnp.concatenate([first, second], 1)


def streamwise(field, inflow):
    extent = field.shape[1]
    padded = padded_2(field, (("gx", 1),), HALO)
    at_inlet = lax.axis_index("gx") == 0
    at_outlet = lax.axis_index("gx") == lax.axis_size("gx") - 1
    ghost_shape = (field.shape[0], HALO) + field.shape[2:]
    lower = jnp.where(at_inlet, jnp.broadcast_to(inflow[:, None], ghost_shape), padded[:, :HALO])
    upper = jnp.where(
        at_outlet, jnp.broadcast_to(field[:, -1:], ghost_shape), padded[:, HALO + extent :]
    )
    padded = jnp.concatenate([lower, field, upper], 1)
    first = jnp.zeros_like(field)
    second = center_coef * field
    for offset in range(1, HALO + 1):
        ahead = padded[:, HALO + offset : HALO + offset + extent]
        behind = padded[:, HALO - offset : HALO - offset + extent]
        first = first + first_coef[offset - 1] * (ahead - behind)
        second = second + second_coef[offset - 1] * (ahead + behind)
    return -(field[0:1] * first) + viscosity * second


def wall_terms(columns, wall_first, wall_second):
    first = jnp.einsum(
        "ij,cxjz->cxiz",
        wall_first,
        columns,
        precision=lax.Precision.HIGHEST,
        preferred_element_type=jnp.float32,
    )
    second = jnp.einsum(
        "ij,cxjz->cxiz",
        wall_second,
        columns,
        precision=lax.Precision.HIGHEST,
        preferred_element_type=jnp.float32,
    )
    return -(columns[1:2] * first) + viscosity * second


def rescale(plane, rows, picks, weight_table):
    levels = jnp.arange(weight_table.shape[0], dtype=jnp.int32)
    frac = jnp.sum(
        jnp.where(picks[:, None] == levels[None, :], weight_table[None, :], 0.0), axis=1
    )[None, :, None]
    lower = jnp.take(plane, rows, axis=1)
    upper = jnp.take(plane, rows + 1, axis=1)
    return (1.0 - frac) * lower + frac * upper


def fetch_recycle(plane):
    count = lax.axis_size("gx")
    return passed_along(plane, "gx", 1 - count)


def shards(
    velocity, accumulated, wall_first, wall_second, recycle_rows, weight_index, weight_table
):
    span = velocity.shape[3]
    rows_here = velocity.shape[2]
    lines = velocity.reshape(-1, span)
    derived = jnp.dot(
        lines,
        spanwise_table(span),
        precision=lax.Precision.HIGHEST,
        preferred_element_type=jnp.float32,
    )
    span_first = derived[:, :span].reshape(velocity.shape)
    span_second = derived[:, span:].reshape(velocity.shape)
    tendency = -(velocity[2:3] * span_first) + viscosity * span_second
    arrived = fetch_recycle(velocity[:, 0])
    whole_plane = lax.all_gather(arrived, "ga", axis=1, tiled=True)
    start = lax.axis_index("ga") * rows_here
    rows = lax.dynamic_slice_in_dim(recycle_rows, start, rows_here)
    picks = lax.dynamic_slice_in_dim(weight_index, start, rows_here)
    inflow = rescale(whole_plane, rows, picks, weight_table)
    tendency = tendency + streamwise(velocity, inflow)
    tendency = tendency + lax.all_to_all(
        wall_terms(
            lax.all_to_all(velocity, "ga", split_axis=3, concat_axis=2, tiled=True),
            wall_first,
            wall_second,
        ),
        "ga",
        split_axis=2,
        concat_axis=3,
        tiled=True,
    )
    accumulated_next = keep_rate * accumulated + step_size * tendency
    return (velocity + update_rate * accumulated_next, accumulated_next)


def solution(mesh):
    in_specs = (P(None, "gx", "ga", None), P(None, "gx", "ga", None), P(), P(), P(), P(), P())
    out_specs = (P(None, "gx", "ga", None), P(None, "gx", "ga", None))
    return jax.shard_map(shards, mesh=mesh, in_specs=in_specs, out_specs=out_specs, check_vma=False)
```

profile of v0, /device:TPU:0, one launch (start us, length us, event | category | flops | bytes accessed | tf_op | source)
XLA Modules:
  0.0 373.6 jit_solution(5462917162191541148)
XLA Ops:
  7.2 0.0 copy-start
  7.2 6.4 %copy.36 = f32[3,4,96,768]{2,1,0,3:T(4,128)} copy(f32[3,4,96,768]{3,2,1,0:T(8,128)} %param.9) | data formatting | bytes 7077888 | tf_op args[0]
  13.6 6.3 %all-to-all-start = ((f32[3,4,96,768]{2,1,0,3:T(4,128)}), f32[3,4,96,768]{2,1,0,3:T(4,128)}, u32[]{:S(2)}, u32[]{:S(2)}) async-start(f32[3,4,96,768]{2,1,0,3:T(4,128)} %copy.36), calls=%async_computation | async-start | bytes 9437184 | tf_op jit(solution)/shard_map/all_to_all | solution.py:139
  19.9 0.0 all-gather.2.cloned.1.call-start
  19.9 2.5 slice_bitcast_fusion.2
  22.4 1.3 collective-permute-start.1
  23.7 14.0 %collective-permute-done.1 = f32[3,96,768]{2,1,0:T(8,128)S(1)} collective-permute-done((f32[3,96,768]{2,1,0:T(8,128)S(1)}, f32[3,96,768]{2,1,0:T(8,128)S(1)}, u32[]{:S(2)}, u32[]{:S(2)}) %collective-permute-start.1) | collective-permute-done | bytes 884768 | tf_op jit(solution)/shard_map/ppermute | solution.py:40
  37.7 0.0 copy-start.4
  37.7 0.9 copy-done.4
  38.6 0.0 all-gather.2.cloned.1.call-update
  38.6 143.0 %all-to-all-done = f32[3,4,96,768]{2,1,0,3:T(4,128)} async-done(((f32[3,4,96,768]{2,1,0,3:T(4,128)}), f32[3,4,96,768]{2,1,0,3:T(4,128)}, u32[]{:S(2)}, u32[]{:S(2)}) %all-to-all-start) | async-done | bytes 3538976 | tf_op jit(solution)/shard_map/all_to_all | solution.py:139
  181.6 7.6 %copy.50 = f32[3,4,96,4,192]{2,3,4,1,0:T(4,128)} copy(f32[3,4,96,4,192]{2,1,0,4,3:T(4,128)} %bitcast.10) | data formatting | bytes 7077888 | tf_op jit(solution)/shard_map/all_to_all | solution.py:139
  189.1 6.2 %all_to_all.29 = f32[3,4,384,192]{2,3,1,0:T(8,128)} reshape(f32[3,4,4,96,192]{3,2,4,1,0:T(4,128)} %bitcast.56) | data formatting | bytes 7077888 | tf_op jit(solution)/shard_map/all_to_all | solution.py:139
  195.3 0.0 copy-done
  195.3 9.5 %fusion.18 = f32[3,4,192,384]{3,2,1,0:T(8,128)} fusion(f32[3,4,384,192]{2,3,1,0:T(8,128)} %all_to_all.29, f32[384,384]{1,0:T(8,128)S(1)} %copy-done), kind=kOutput, calls=%fused_computation.56 | convolution fusion | flops 4076863488 | bytes 7667712 | tf_op jit(solution)/shard_map/ij,cxjz->cxiz/dot_general | solution.py:90
  204.9 1.6 slice.73
  206.5 0.8 mul.198
  207.2 0.0 copy-done.5
  207.3 10.2 %bitcast_add_fusion = f32[3,4,384,192]{2,3,1,0:T(8,128)} fusion(f32[3,4,192,384]{3,2,1,0:T(8,128)} %fusion.18, f32[3,4,384,192]{2,3,1,0:T(8,128)} %all_to_all.29, f32[4,384,192]{1,2,0:T(8,128)S(1)} %mul.198, f32[384,384]{1,0:T(8,128)S(1)} %copy-done.5), kind=kOutput, calls=%fused_computation.22 | convolution fusion | flops 4080402432 | bytes 12386304 | tf_op jit(solution)/shard_map/ij,cxjz->cxiz/dot_general | solution.py:83
  217.5 6.7 %copy.38 = f32[3,4,384,192]{3,1,0,2:T(4,128)} copy(f32[3,4,384,192]{2,3,1,0:T(8,128)} %bitcast_add_fusion) | data formatting | bytes 7077888 | tf_op jit(solution)/shard_map/add | solution.py:97
  224.2 5.1 %all-to-all-start.1 = ((f32[3,4,384,192]{3,1,0,2:T(4,128)}), f32[3,4,384,192]{3,1,0,2:T(4,128)}, u32[]{:S(2)}, u32[]{:S(2)}) async-start(f32[3,4,384,192]{3,1,0,2:T(4,128)} %copy.38), calls=%async_computation.1 | async-start | bytes 9437184 | tf_op jit(solution)/shard_map/all_to_all | solution.py:137
  229.3 1.3 collective-permute-start
  230.6 5.0 %collective-permute-start.2 = (f32[3,4,96,768]{3,2,1,0:T(8,128)}, f32[3,4,96,768]{3,2,1,0:T(8,128)}, u32[]{:S(2)}, u32[]{:S(2)}) collective-permute-start(f32[3,4,96,768]{3,2,1,0:T(8,128)} %param.9), channel_id=1, source_target_pairs={{0,4},{4,8},{8,12},{12,16},{16,20},{20,24},{24,28},{1,5},{5,9},{9,... | collective-permute-start | bytes 10616840 | tf_op jit(solution)/shard_map/ppermute | solution.py:28
  235.7 0.8 dynamic_slice.6
  236.5 0.8 compare_and_fusion.1
  237.2 0.0 copy-done.6
  237.2 0.1 select_reduce_fusion
  237.3 1.9 slice_bitcast_fusion.1
  239.2 0.0 copy-start.2
  239.2 11.5 %divide_select_fusion = (f32[768,768]{1,0:T(8,128)S(1)}, f32[768,768]{1,0:T(8,128)S(1)}) fusion(), kind=kLoop, calls=%fused_computation.36 | loop fusion | flops 20643840 | bytes 4718592 | tf_op jit(solution)/shard_map/jit(_where)/select_n | solution.py:53
  250.7 0.0 copy-done.2
  250.7 19.1 %convolution_bitcast_fusion = f32[1152,1536]{1,0:T(8,128)S(1)} fusion(f32[1152,768]{1,0:T(8,128)S(1)} %bitcast.55, f32[768,768]{1,0:T(8,128)S(1)} %get-tuple-element.19, f32[768,768]{1,0:T(8,128)S(1)} %get-tuple-element.20), kind=kOutput, calls=%fused_computation.2 | convolution fusion | flops 16308633600 | bytes 15335424 | tf_op jit(solution)/shard_map/dot_general | solution.py:121
  269.8 0.0 copy-start.3
  269.8 3.4 fusion.22
  273.2 0.0 collective-permute-done
  273.2 0.0 copy-done.3
  273.2 4.1 %broadcast_select_fusion.1 = f32[3,4,96,768]{3,2,1,0:T(8,128)} fusion(f32[3,4,96,768]{3,2,1,0:T(8,128)} %collective-permute-done, f32[3,96,768]{2,1,0:T(8,128)S(1)} %copy-done.3, pred[]{:T(512)S(6)} %eq.29), kind=kLoop, calls=%fused_computation.46 | loop fusion | flops 884736 | bytes 7962625 | tf_op jit(solution)/shard_map/jit(_where)/select_n | solution.py:68
  277.3 6.7 %copy.32 = f32[3,384,768]{2,0,1:T(4,128)} copy(f32[3,384,768]{2,1,0:T(8,128)} %all-gather.2.cloned.1.call-done) | data formatting | bytes 7077888 | tf_op jit(solution)/shard_map/all_gather | solution.py:131
  283.9 4.6 %gather_fusion = f32[96,3,768]{2,1,0:T(4,128)} fusion(f32[3,384,768]{2,0,1:T(4,128)} %copy.32, s32[1024]{0:T(1024)S(1)} %get-tuple-element.18), kind=kCustom, calls=%fused_computation.clone | custom fusion | bytes 1769856 | tf_op jit(solution)/shard_map/jit(_take)/gather | solution.py:105
  288.6 4.6 %gather_fusion.1 = f32[96,3,768]{2,1,0:T(4,128)} fusion(f32[3,384,768]{2,0,1:T(4,128)} %copy.32, s32[1024]{0:T(1024)S(1)} %get-tuple-element.17), kind=kCustom, calls=%fused_computation.1.clone | custom fusion | bytes 1769856 | tf_op jit(solution)/shard_map/jit(_take)/gather | solution.py:106
  293.2 2.1 fusion.17
  295.3 0.0 collective-permute-done.2
  295.3 2.1 broadcast_select_fusion
  297.3 35.9 %all-to-all-done.1 = f32[3,4,384,192]{3,1,0,2:T(4,128)} async-done(((f32[3,4,384,192]{3,1,0,2:T(4,128)}), f32[3,4,384,192]{3,1,0,2:T(4,128)}, u32[]{:S(2)}, u32[]{:S(2)}) %all-to-all-start.1) | async-done | bytes 3538976 | tf_op jit(solution)/shard_map/all_to_all | solution.py:137
  333.2 7.7 %copy.39 = f32[3,4,96,4,192]{4,3,2,1,0:T(4,128)} copy(f32[3,4,96,4,192]{4,1,0,2,3:T(4,128)} %bitcast.19) | data formatting | bytes 7077888 | tf_op jit(solution)/shard_map/all_to_all | solution.py:137
  341.0 6.0 %all_to_all.33 = f32[3,4,96,768]{3,2,1,0:T(8,128)} reshape(f32[3,4,96,4,192]{4,3,2,1,0:T(4,128)} %copy.39) | data formatting | bytes 7077888 | tf_op jit(solution)/shard_map/all_to_all | solution.py:137
  347.0 19.5 %multiply_add_fusion = (f32[3,4,96,768]{3,2,1,0:T(8,128)}, f32[3,4,96,768]{3,2,1,0:T(8,128)}) fusion(f32[3,4,96,768]{3,2,1,0:T(8,128)} %param.9, f32[3,4,96,768]{3,2,1,0:T(8,128)} %all_to_all.33, f32[3,4,96,768]{3,2,1,0:T(8,128)} %broadcast_select_fusion.1, f32[3,4,96,768]{3,2,1,0:T(8,128)} %broadcast_select_fusion, f32[4,96,768]{2,1,0:T(8,128)S(1)} %get-tuple-element.12, ...), kind=kLoop, calls=%fused_computation.25 | loop fusion | flops 38928384 | bytes 34209792 | tf_op jit(solution)/shard_map/add | solution.py:149
  366.5 0.0 copy-done.1
  (6 shorter events, 0.0 us)
Async XLA Ops:
  7.2 188.2 %copy-start = (f32[384,384]{1,0:T(8,128)S(1)}, f32[384,384]{1,0:T(8,128)}, u32[]{:S(2)}) copy-start(f32[384,384]{1,0:T(8,128)} %param.12) | copy-start | bytes 1769476
  13.6 168.0 %all-to-all-start = ((f32[3,4,96,768]{2,1,0,3:T(4,128)}), f32[3,4,96,768]{2,1,0,3:T(4,128)}, u32[]{:S(2)}, u32[]{:S(2)}) async-start(f32[3,4,96,768]{2,1,0,3:T(4,128)} %copy.36), calls=%async_computation | async-start | bytes 9437184 | tf_op jit(solution)/shard_map/all_to_all | solution.py:139
  19.9 257.4 %all-gather.2.cloned.1.call-start = ((), (), s32[]{:S(2)}) async-start(), calls=%async_computation.2 | async-start | bytes 4423680 | tf_op jit(solution)/shard_map/all_gather | solution.py:131
  22.4 15.2 %collective-permute-start.1 = (f32[3,96,768]{2,1,0:T(8,128)S(1)}, f32[3,96,768]{2,1,0:T(8,128)S(1)}, u32[]{:S(2)}, u32[]{:S(2)}) collective-permute-start(f32[3,96,768]{2,1,0:T(8,128)S(1)} %get-tuple-element.13), channel_id=1, source_target_pairs={{28,0},{29,1},{30,2},{31,3}} | collective-permute-start | bytes 2654216 | tf_op jit(solution)/shard_map/ppermute | solution.py:40
  37.7 0.9 copy-start.4
  204.9 2.4 copy-start.5
  224.2 13.0 %copy-start.6 = (f32[64]{0:T(128)S(1)}, f32[64]{0:T(128)}, u32[]{:S(2)}) copy-start(f32[64]{0:T(128)} %param.15) | copy-start | bytes 772
  224.2 109.0 %all-to-all-start.1 = ((f32[3,4,384,192]{3,1,0,2:T(4,128)}), f32[3,4,384,192]{3,1,0,2:T(4,128)}, u32[]{:S(2)}, u32[]{:S(2)}) async-start(f32[3,4,384,192]{3,1,0,2:T(4,128)} %copy.38), calls=%async_computation.1 | async-start | bytes 9437184 | tf_op jit(solution)/shard_map/all_to_all | solution.py:137
  229.3 43.9 %collective-permute-start = (f32[3,4,96,768]{3,2,1,0:T(8,128)}, f32[3,4,96,768]{3,2,1,0:T(8,128)}, u32[]{:S(2)}, u32[]{:S(2)}) collective-permute-start(f32[3,4,96,768]{3,2,1,0:T(8,128)} %param.9), channel_id=1, source_target_pairs={{4,0},{8,4},{12,8},{16,12},{20,16},{24,20},{28,24},{5,1},{9,5},{13... | collective-permute-start | bytes 10616840 | tf_op jit(solution)/shard_map/ppermute | solution.py:30
  230.6 64.6 %collective-permute-start.2 = (f32[3,4,96,768]{3,2,1,0:T(8,128)}, f32[3,4,96,768]{3,2,1,0:T(8,128)}, u32[]{:S(2)}, u32[]{:S(2)}) collective-permute-start(f32[3,4,96,768]{3,2,1,0:T(8,128)} %param.9), channel_id=1, source_target_pairs={{0,4},{4,8},{8,12},{12,16},{16,20},{20,24},{24,28},{1,5},{5,9},{9,... | collective-permute-start | bytes 10616840 | tf_op jit(solution)/shard_map/ppermute | solution.py:28
  239.2 11.5 %copy-start.2 = (f32[3,4,96,768]{3,2,1,0:T(8,128)S(1)}, f32[3,4,96,768]{3,2,1,0:T(8,128)}, u32[]{:S(2)}) copy-start(f32[3,4,96,768]{3,2,1,0:T(8,128)} %param.9) | copy-start | bytes 10616836
  269.8 3.4 copy-start.3
  347.0 19.5 %copy-start.1 = (f32[384,384]{1,0:T(8,128)S(1)}, f32[384,384]{1,0:T(8,128)}, u32[]{:S(2)}) copy-start(f32[384,384]{1,0:T(8,128)} %param.12) | copy-start | bytes 1769476
Sparse Core Ops, SparseCore 0:
  38.7 118.2 all-gather.1
where the time goes:
time: 378 us; the launch traced here: 374 us
  waiting for transfers between devices  193 us (51%)
  local copies, waits for them, and re-layouts  65 us (17%)
  other arithmetic  43.5 us (12%)
  matrix products  38.8 us (10%)
  starting transfers between devices  19 us (5%)
  between operations  14.4 us (4%)
    all_to_all x1, waiting for transfers between devices, shards(): lax.all_to_all(velocity, 'ga', split_axis=3, concat_axis=2, tiled=True)  143 us
    all_to_all x1, waiting for transfers between devices, shards(): lax.all_to_all(wall_terms(lax.all_to_all(velocity, 'ga', split_axis=3, co...  35.9 us
    add x1, other arithmetic, shards(): return (velocity + update_rate * accumulated_next, accumulated_next)  19.5 us
    dot_general x1, matrix products, shards(): jnp.dot(lines, spanwise_table(span), precision=lax.Precision.HIGHEST, pre...  19.1 us
    ppermute x1, waiting for transfers between devices, passed_along(): return lax.ppermute(shard, axis, pairs)  14 us
    all_to_all x2, local copies, waits for them, and re-layouts, shards(): lax.all_to_all(velocity, 'ga', split_axis=3, concat_axis=2, tiled=True)  13.8 us
    all_to_all x2, local copies, waits for them, and re-layouts, shards(): lax.all_to_all(wall_terms(lax.all_to_all(velocity, 'ga', split_axis=3, co...  13.8 us
    select_n x1, other arithmetic, spanwise_table(): jnp.where(same, -math.pi * math.pi / 3.0 - spacing * spacing / 6.0, -0.5...  11.5 us
  transfers between devices with their start and end apart: 6, of which 3 were waited for; matrix products, arithmetic and copies ran while one was open for 27% of the time, Pallas kernels for 0%

commit v1 on v0

--- a/solution.py
+++ b/solution.py
@@ -1,8 +1,12 @@
+import functools
 import math
 
 import jax
 import jax.numpy as jnp
+import numpy as np
 from jax import lax
+from jax.experimental import pallas as pl
+from jax.experimental.pallas import tpu as pltpu
 from jax.sharding import PartitionSpec as P
 
 HALO = 4
@@ -97,14 +101,23 @@
     return -(columns[1:2] * first) + viscosity * second
 
 
-def rescale(plane, rows, picks, weight_table):
+def interpolation(rows, picks, weight_table, height):
     levels = jnp.arange(weight_table.shape[0], dtype=jnp.int32)
     frac = jnp.sum(
         jnp.where(picks[:, None] == levels[None, :], weight_table[None, :], 0.0), axis=1
-    )[None, :, None]
-    lower = jnp.take(plane, rows, axis=1)
-    upper = jnp.take(plane, rows + 1, axis=1)
-    return (1.0 - frac) * lower + frac * upper
+    )[:, None]
+    apart = jnp.arange(height, dtype=jnp.int32)[None, :] - rows[:, None]
+    return jnp.where(apart == 0, 1.0 - frac, jnp.where(apart == 1, frac, 0.0))
+
+
+def rescale(plane, rows, picks, weight_table):
+    return jnp.einsum(
+        "ij,cjz->ciz",
+        interpolation(rows, picks, weight_table, plane.shape[1]),
+        plane,
+        precision=lax.Precision.HIGHEST,
+        preferred_element_type=jnp.float32,
+    )
 
 
 def fetch_recycle(plane):
@@ -149,7 +162,384 @@
     return (velocity + update_rate * accumulated_next, accumulated_next)
 
 
+MESH = pl.DeviceIdType.MESH
+PARTS = 3
+
+
+def folded_tables(length):
+    half = length // 2
+    apart = np.arange(length)[None, :] - np.arange(length)[:, None]
+    apart = np.remainder(apart + half, length) - half
+    parity = 1.0 - 2.0 * np.remainder(apart, 2)
+    spacing = 2.0 * math.pi / length
+    angle = apart * (0.5 * spacing)
+    same = apart == 0
+    sine = np.where(same, 1.0, np.sin(angle))
+    first = np.where(same, 0.0, 0.5 * spacing * parity * np.cos(angle) / sine)
+    first = np.where(np.abs(apart) == half, 0.0, first)
+    second = np.where(
+        same,
+        -math.pi * math.pi / 3.0 - spacing * spacing / 6.0,
+        -0.5 * spacing * spacing * parity / (sine * sine),
+    )
+    near = np.concatenate([first[:half, :half], second[:half, :half]], 1)
+    far = np.concatenate([first[half:, :half], second[half:, :half]], 1)
+    return (
+        (0.5 * (near + far)).astype(np.float32),
+        (0.5 * (near - far)).astype(np.float32),
+    )
+
+
+def exact_dot(left, right):
+    return jnp.dot(
+        left, right, precision=lax.Precision.HIGHEST, preferred_element_type=jnp.float32
+    )
+
+
+def section_kernel(
+    slabs,
+    group,
+    vel,
+    acc,
+    wall,
+    mix,
+    even,
+    odd,
+    vel_out,
+    acc_out,
+    gath,
+    ret_src,
+    ret_in,
+    tend,
+    lo,
+    hi,
+    inf_src,
+    fwd_send,
+    fwd_recv,
+    ret_send,
+    ret_recv,
+    lo_send,
+    lo_recv,
+    hi_send,
+    hi_recv,
+    inf_send,
+    inf_recv,
+):
+    gx = lax.axis_index("gx")
+    me = lax.axis_index("ga")
+    planes, rows, span = vel.shape[1:]
+    width = span // PARTS
+    half = span // 2
+    height = group * rows
+    chunks = 3 * PARTS
+    not_first = gx > 0
+    not_last = gx < slabs - 1
+    source = jnp.logical_and(gx == slabs - 1, me == 0)
+
+    def place(t):
+        turn = t // PARTS
+        c = lax.rem(1 + 2 * turn, 3)
+        lanes = pl.ds(pl.multiple_of((t - turn * PARTS) * width, width), width)
+        return c, lanes
+
+    def fwd(t, d):
+        c, lanes = place(t)
+        peer = lax.rem(me + d, group)
+        return pltpu.make_async_remote_copy(
+            src_ref=vel.at[c, peer, :, lanes],
+            dst_ref=gath.at[c, me, :, lanes],
+            send_sem=fwd_send.at[t, d - 1],
+            recv_sem=fwd_recv.at[t, d - 1],
+            device_id={"ga": peer},
+            device_id_type=MESH,
+        )
+
+    def ret(t, d):
+        c, lanes = place(t)
+        peer = lax.rem(me + d, group)
+        return pltpu.make_async_remote_copy(
+            src_ref=ret_src.at[c, peer, :, lanes],
+            dst_ref=ret_in.at[c, me, :, lanes],
+            send_sem=ret_send.at[t, d - 1],
+            recv_sem=ret_recv.at[t, d - 1],
+            device_id={"ga": peer},
+            device_id_type=MESH,
+        )
+
+    def inf(t, k):
+        c, lanes = place(t)
+        return pltpu.make_async_remote_copy(
+            src_ref=inf_src.at[c, k, :, lanes],
+            dst_ref=lo.at[c, 0, :, lanes],
+            send_sem=inf_send.at[t, k],
+            recv_sem=inf_recv.at[t],
+            device_id={"gx": 0, "ga": k},
+            device_id_type=MESH,
+        )
+
+    def upward(c):
+        return pltpu.make_async_remote_copy(
+            src_ref=vel.at[c],
+            dst_ref=lo.at[c],
+            send_sem=lo_send.at[c],
+            recv_sem=lo_recv.at[c],
+            device_id={"gx": lax.rem(gx + 1, slabs)},
+            device_id_type=MESH,
+        )
+
+    def downward(c):
+        return pltpu.make_async_remote_copy(
+            src_ref=vel.at[c],
+            dst_ref=hi.at[c],
+            send_sem=hi_send.at[c],
+            recv_sem=hi_recv.at[c],
+            device_id={"gx": lax.rem(gx + slabs - 1, slabs)},
+            device_id_type=MESH,
+        )
+
+    barrier = pltpu.get_barrier_semaphore()
+    for d in range(1, group):
+        pl.semaphore_signal(
+            barrier, inc=1, device_id={"ga": lax.rem(me + d, group)}, device_id_type=MESH
+        )
+
+    @pl.when(not_first)
+    def _():
+        pl.semaphore_signal(barrier, inc=1, device_id={"gx": gx - 1}, device_id_type=MESH)
+
+    @pl.when(not_last)
+    def _():
+        pl.semaphore_signal(barrier, inc=1, device_id={"gx": gx + 1}, device_id_type=MESH)
+
+    @pl.when(gx == 0)
+    def _():
+        pl.semaphore_signal(
+            barrier, inc=1, device_id={"gx": slabs - 1, "ga": 0}, device_id_type=MESH
+        )
+
+    @pl.when(source)
+    def _():
+        for k in range(group):
+            pl.semaphore_signal(
+                barrier, inc=1, device_id={"gx": 0, "ga": k}, device_id_type=MESH
+            )
+
+    expected = (
+        group
+        - 1
+        + not_first.astype(jnp.int32)
+        + not_last.astype(jnp.int32)
+        + (gx == 0).astype(jnp.int32)
+        + group * source.astype(jnp.int32)
+    )
+    pl.semaphore_wait(barrier, expected)
+
+    def send_fwd(t, carry):
+        for d in range(1, group):
+            fwd(t, d).start()
+        return carry
+
+    lax.fori_loop(0, PARTS, send_fwd, 0)
+    for c in range(3):
+
+        @pl.when(not_last)
+        def _():
+            upward(c).start()
+
+        @pl.when(not_first)
+        def _():
+            downward(c).start()
+
+    lax.fori_loop(PARTS, chunks, send_fwd, 0)
+
+    for c in range(3):
+        gath[c, me] = vel[c, me]
+
+    @pl.when(jnp.logical_not(not_last))
+    def _():
+        for c in range(3):
+            hi[c, 0] = vel[c, planes - 1]
+
+    def spanwise_step(c, carry):
+        left = vel[c, :, :, :half].reshape(planes * rows, half)
+        right = vel[c, :, :, half:].reshape(planes * rows, half)
+        sums = exact_dot(left + right, even[...])
+        differences = exact_dot(left - right, odd[...])
+        for side in range(2):
+            both = sums + differences if side == 0 else sums - differences
+            lanes = slice(side * half, (side + 1) * half)
+            first = both[:, :half].reshape(planes, rows, half)
+            second = both[:, half:].reshape(planes, rows, half)
+            tend[c, :, :, lanes] = viscosity * second - vel[2, :, :, lanes] * first
+        return carry
+
+    lax.fori_loop(0, 3, spanwise_step, 0)
+
+    def wall_step(t, carry):
+        c, lanes = place(t)
+        for d in range(1, group):
+            fwd(t, d).wait_recv()
+        columns = gath[c, :, :, lanes].reshape(height, width)
+        normal = gath[1, :, :, lanes].reshape(height, width)
+        both = exact_dot(wall[...], columns)
+        term = viscosity * both[height:] - normal * both[:height]
+        ret_src[c, :, :, lanes] = term.reshape(group, rows, width)
+        for d in range(1, group):
+            ret(t, d).start()
+        ret_in[c, me, :, lanes] = ret_src[c, me, :, lanes]
+
+        @pl.when(source)
+        def _():
+            mixed = exact_dot(mix[...], columns)
+            inf_src[c, :, :, lanes] = mixed.reshape(group, rows, width)
+            for k in range(group):
+                inf(t, k).start()
+
+        return carry
+
+    lax.fori_loop(0, chunks, wall_step, 0)
+
+    def stream_step(turn, carry):
+        c = lax.rem(1 + 2 * turn, 3)
+
+        @pl.when(not_first)
+        def _():
+            upward(c).wait_recv()
+
+        @pl.when(gx == 0)
+        def _():
+            for part in range(PARTS):
+                inf(turn * PARTS + part, 0).wait_recv()
+
+        @pl.when(not_last)
+        def _():
+            downward(c).wait_recv()
+
+        def tile(i, inner):
+            block = i // PARTS
+            where = pl.ds(pl.multiple_of(block * 8, 8), 8)
+            lanes = pl.ds(pl.multiple_of((i - block * PARTS) * width, width), width)
+            line = [
+                lo[c, p * not_first.astype(jnp.int32), where, lanes] for p in range(HALO)
+            ]
+            line += [vel[c, p, where, lanes] for p in range(planes)]
+            line += [hi[c, p * not_last.astype(jnp.int32), where, lanes] for p in range(HALO)]
+            for x in range(planes):
+                middle = x + HALO
+                first = None
+                second = center_coef * line[middle]
+                for m in range(1, HALO + 1):
+                    ahead, behind = line[middle + m], line[middle - m]
+                    step = first_coef[m - 1] * (ahead - behind)
+                    first = step if first is None else first + step
+                    second = second + second_coef[m - 1] * (ahead + behind)
+                total = viscosity * second - vel[0, x, where, lanes] * first
+                tend[c, x, where, lanes] = tend[c, x, where, lanes] + total
+            return inner
+
+        lax.fori_loop(0, rows // 8 * PARTS, tile, 0)
+        return carry
+
+    lax.fori_loop(0, 3, stream_step, 0)
+
+    def last_step(t, carry):
+        c, lanes = place(t)
+        for d in range(1, group):
+            ret(t, d).wait_recv()
+        tendency = tend[c, :, :, lanes] + ret_in[c, :, :, lanes]
+        following = keep_rate * acc[c, :, :, lanes] + step_size * tendency
+        acc_out[c, :, :, lanes] = following
+        vel_out[c, :, :, lanes] = vel[c, :, :, lanes] + update_rate * following
+        return carry
+
+    lax.fori_loop(0, chunks, last_step, 0)
+
+    def drain(t, carry):
+        for d in range(1, group):
+            fwd(t, d).wait_send()
+            ret(t, d).wait_send()
+
+        @pl.when(source)
+        def _():
+            for k in range(group):
+                inf(t, k).wait_send()
+
+        return carry
+
+    lax.fori_loop(0, chunks, drain, 0)
+    for c in range(3):
+
+        @pl.when(not_last)
+        def _():
+            upward(c).wait_send()
+
+        @pl.when(not_first)
+        def _():
+            downward(c).wait_send()
+
+
+def fast_shards(
+    slabs,
+    group,
+    velocity,
+    accumulated,
+    wall_first,
+    wall_second,
+    recycle_rows,
+    weight_index,
+    weight_table,
+):
+    _, planes, rows, span = velocity.shape
+    height = rows * group
+    chunks = 3 * PARTS
+    even, odd = folded_tables(span)
+    wall = jnp.concatenate([wall_first, wall_second], 0)
+    mix = interpolation(recycle_rows, weight_index, weight_table, height)
+    whole = pl.BlockSpec(memory_space=pltpu.VMEM)
+    shape = jax.ShapeDtypeStruct(velocity.shape, jnp.float32)
+    dma = pltpu.SemaphoreType.DMA
+    slab = pltpu.VMEM((3, planes, rows, span), jnp.float32)
+    exchanged = pltpu.VMEM((3, group, rows, span), jnp.float32)
+    halo = pltpu.VMEM((3, HALO, rows, span), jnp.float32)
+    return pl.pallas_call(
+        functools.partial(section_kernel, slabs, group),
+        out_shape=(shape, shape),
+        in_specs=[whole] * 6,
+        out_specs=(whole, whole),
+        scratch_shapes=[
+            exchanged,
+            exchanged,
+            slab,
+            slab,
+            halo,
+            halo,
+            exchanged,
+            dma((chunks, group - 1)),
+            dma((chunks, group - 1)),
+            dma((chunks, group - 1)),
+            dma((chunks, group - 1)),
+            dma((3,)),
+            dma((3,)),
+            dma((3,)),
+            dma((3,)),
+            dma((chunks, group)),
+            dma((chunks,)),
+        ],
+        compiler_params=pltpu.CompilerParams(
+            collective_id=0, has_side_effects=True, vmem_limit_bytes=60 * 1024 * 1024
+        ),
+    )(velocity, accumulated, wall, mix, jnp.asarray(even), jnp.asarray(odd))
+
+
 def solution(mesh):
     in_specs = (P(None, "gx", "ga", None), P(None, "gx", "ga", None), P(), P(), P(), P(), P())
     out_specs = (P(None, "gx", "ga", None), P(None, "gx", "ga", None))
-    return jax.shard_map(shards, mesh=mesh, in_specs=in_specs, out_specs=out_specs, check_vma=False)
+    slabs, group = mesh.shape["gx"], mesh.shape["ga"]
+
+    def body(velocity, *others):
+        _, planes, rows, span = velocity.shape
+        if planes == HALO == group and slabs > 2 and rows % 8 == 0 and span % 768 == 0:
+            return fast_shards(slabs, group, velocity, *others)
+        return shards(velocity, *others)
+
+    return jax.shard_map(body, mesh=mesh, in_specs=in_specs, out_specs=out_specs, check_vma=False)

time: 378 us -> 195 us (0.52)
  the two profiles are of different devices: /device:TPU:0 before, /device:TPU:30 now
where the time goes in v1:
time: 195 us
  Pallas kernels  183 us (94%)
  local copies, waits for them, and re-layouts  5.97 us (3%)
  other arithmetic  4.85 us (2%)
    pallas_call x1, Pallas kernels, fast_shards(): pl.pallas_call(functools.partial(section_kernel, slabs, group), out_shape...  183 us
    unnamed x4, local copies, waits for them, and re-layouts  5.97 us

profile of v1, /device:TPU:30, one launch (start us, length us, event | category | flops | bytes accessed | tf_op | source)
XLA Modules:
  0.0 194.7 jit_solution(10451025827800680116)
XLA Ops:
  0.6 0.8 select_reduce_fusion
  1.4 1.7 select_select_fusion.mix
  3.1 2.3 %pad_maximum_fusion.wall = f32[768,384]{1,0:T(8,128)} fusion(f32[384,384]{1,0:T(8,128)} %param.12, f32[384,384]{1,0:T(8,128)} %param.11), kind=kLoop, calls=%fused_computation | loop fusion | flops 294912 | bytes 2359296 | tf_op jit(solution)/shard_map/concatenate | solution.py:496
  5.5 183.3 %shard_map.104 = (f32[3,4,96,768]{3,2,1,0:T(8,128)}, f32[3,4,96,768]{3,2,1,0:T(8,128)}) custom-call(f32[3,4,96,768]{3,2,1,0:T(8,128)} %vel.1, f32[3,4,96,768]{3,2,1,0:T(8,128)} %acc.1, f32[768,384]{1,0:T(8,128)} %pad_maximum_fusion.wall, f32[384,384]{1,0:T(8,128)} %select_select_fusion.mix, f32[384,768]{1,0:T(8,128)} %constant.12.clone.even, ...), custom_call_target="tpu_custom_call" | custom-call | tf_op jit(solution)/shard_map/pallas_call | solution.py:504
  188.7 0.0 copy-start
  188.8 4.2 %copy.13 = f32[3,4,96,768]{3,2,1,0:T(8,128)} copy(f32[3,4,96,768]{3,2,1,0:T(8,128)} %get-tuple-element.4) | data formatting | bytes 7077888
  192.9 0.0 copy-done
  192.9 1.8 copy.14
  (1 shorter events, 0.0 us)
Async XLA Ops:
  188.7 4.2 %copy-start = (f32[3,4,96,768]{3,2,1,0:T(8,128)S(1)}, f32[3,4,96,768]{3,2,1,0:T(8,128)}, u32[]{:S(2)}) copy-start(f32[3,4,96,768]{3,2,1,0:T(8,128)} %get-tuple-element.5) | copy-start | bytes 10616836

commit v2 on v1

--- a/solution.py
+++ b/solution.py
@@ -163,7 +163,9 @@
 
 
 MESH = pl.DeviceIdType.MESH
-PARTS = 3
+PARTS = 2
+TILE = 256
+SHIFTS = 2
 
 
 def folded_tables(length):
@@ -199,18 +201,23 @@
 def section_kernel(
     slabs,
     group,
+    vel_hbm,
+    first_hbm,
+    second_hbm,
+    even_hbm,
+    odd_hbm,
+    entries,
+    picks,
+    table,
+    tend,
     vel,
-    acc,
     wall,
-    mix,
     even,
     odd,
-    vel_out,
-    acc_out,
+    mix,
     gath,
     ret_src,
     ret_in,
-    tend,
     lo,
     hi,
     inf_src,
@@ -224,6 +231,7 @@
     hi_recv,
     inf_send,
     inf_recv,
+    load_sem,
 ):
     gx = lax.axis_index("gx")
     me = lax.axis_index("ga")
@@ -234,7 +242,17 @@
     chunks = 3 * PARTS
     not_first = gx > 0
     not_last = gx < slabs - 1
-    source = jnp.logical_and(gx == slabs - 1, me == 0)
+    last = gx == slabs - 1
+    source = jnp.logical_and(last, jnp.logical_and(me >= 1, me <= SHIFTS))
+    loads = [pltpu.make_async_copy(vel_hbm.at[c], vel.at[c], load_sem.at[c]) for c in range(3)]
+    loads += [
+        pltpu.make_async_copy(even_hbm, even, load_sem.at[3]),
+        pltpu.make_async_copy(odd_hbm, odd, load_sem.at[4]),
+        pltpu.make_async_copy(first_hbm, wall.at[pl.ds(0, height)], load_sem.at[5]),
+        pltpu.make_async_copy(second_hbm, wall.at[pl.ds(height, height)], load_sem.at[6]),
+    ]
+    for load in loads:
+        load.start()
 
     def place(t):
         turn = t // PARTS
@@ -242,11 +260,17 @@
         lanes = pl.ds(pl.multiple_of((t - turn * PARTS) * width, width), width)
         return c, lanes
 
+    def shift(t):
+        return 1 + lax.rem(t - (t // PARTS) * PARTS, SHIFTS)
+
+    def plane_of(device, t):
+        return lax.rem(device - shift(t) + group, group)
+
     def fwd(t, d):
         c, lanes = place(t)
         peer = lax.rem(me + d, group)
         return pltpu.make_async_remote_copy(
-            src_ref=vel.at[c, peer, :, lanes],
+            src_ref=vel_hbm.at[c, plane_of(peer, t), :, lanes],
             dst_ref=gath.at[c, me, :, lanes],
             send_sem=fwd_send.at[t, d - 1],
             recv_sem=fwd_recv.at[t, d - 1],
@@ -259,7 +283,7 @@
         peer = lax.rem(me + d, group)
         return pltpu.make_async_remote_copy(
             src_ref=ret_src.at[c, peer, :, lanes],
-            dst_ref=ret_in.at[c, me, :, lanes],
+            dst_ref=ret_in.at[c, plane_of(me, t), :, lanes],
             send_sem=ret_send.at[t, d - 1],
             recv_sem=ret_recv.at[t, d - 1],
             device_id={"ga": peer},
@@ -279,7 +303,7 @@
 
     def upward(c):
         return pltpu.make_async_remote_copy(
-            src_ref=vel.at[c],
+            src_ref=vel_hbm.at[c],
             dst_ref=lo.at[c],
             send_sem=lo_send.at[c],
             recv_sem=lo_recv.at[c],
@@ -289,7 +313,7 @@
 
     def downward(c):
         return pltpu.make_async_remote_copy(
-            src_ref=vel.at[c],
+            src_ref=vel_hbm.at[c],
             dst_ref=hi.at[c],
             send_sem=hi_send.at[c],
             recv_sem=hi_recv.at[c],
@@ -313,9 +337,10 @@
 
     @pl.when(gx == 0)
     def _():
-        pl.semaphore_signal(
-            barrier, inc=1, device_id={"gx": slabs - 1, "ga": 0}, device_id_type=MESH
-        )
+        for k in range(1, SHIFTS + 1):
+            pl.semaphore_signal(
+                barrier, inc=1, device_id={"gx": slabs - 1, "ga": k}, device_id_type=MESH
+            )
 
     @pl.when(source)
     def _():
@@ -329,7 +354,7 @@
         - 1
         + not_first.astype(jnp.int32)
         + not_last.astype(jnp.int32)
-        + (gx == 0).astype(jnp.int32)
+        + SHIFTS * (gx == 0).astype(jnp.int32)
         + group * source.astype(jnp.int32)
     )
     pl.semaphore_wait(barrier, expected)
@@ -352,8 +377,17 @@
 
     lax.fori_loop(PARTS, chunks, send_fwd, 0)
 
-    for c in range(3):
-        gath[c, me] = vel[c, me]
+    for load in loads:
+        load.wait()
+
+    @pl.when(source)
+    def _():
+        levels = lax.broadcasted_iota(jnp.int32, (table.shape[1], height), 0)
+        chosen = jnp.where(levels == picks[...], 1.0, 0.0)
+        frac = exact_dot(jnp.broadcast_to(table[...], (8, table.shape[1])), chosen)[:1]
+        apart = lax.broadcasted_iota(jnp.int32, (height, height), 0) - entries[...]
+        upright = jnp.where(apart == 0, 1.0 - frac, jnp.where(apart == 1, frac, 0.0))
+        mix[...] = upright.T
 
     @pl.when(jnp.logical_not(not_last))
     def _():
@@ -379,6 +413,7 @@
         c, lanes = place(t)
         for d in range(1, group):
             fwd(t, d).wait_recv()
+        gath[c, me, :, lanes] = vel[c, plane_of(me, t), :, lanes]
         columns = gath[c, :, :, lanes].reshape(height, width)
         normal = gath[1, :, :, lanes].reshape(height, width)
         both = exact_dot(wall[...], columns)
@@ -386,9 +421,9 @@
         ret_src[c, :, :, lanes] = term.reshape(group, rows, width)
         for d in range(1, group):
             ret(t, d).start()
-        ret_in[c, me, :, lanes] = ret_src[c, me, :, lanes]
-
-        @pl.when(source)
+        ret_in[c, plane_of(me, t), :, lanes] = ret_src[c, me, :, lanes]
+
+        @pl.when(jnp.logical_and(last, me == shift(t)))
         def _():
             mixed = exact_dot(mix[...], columns)
             inf_src[c, :, :, lanes] = mixed.reshape(group, rows, width)
@@ -416,9 +451,9 @@
             downward(c).wait_recv()
 
         def tile(i, inner):
-            block = i // PARTS
+            block = i // (span // TILE)
             where = pl.ds(pl.multiple_of(block * 8, 8), 8)
-            lanes = pl.ds(pl.multiple_of((i - block * PARTS) * width, width), width)
+            lanes = pl.ds(pl.multiple_of((i - block * (span // TILE)) * TILE, TILE), TILE)
             line = [
                 lo[c, p * not_first.astype(jnp.int32), where, lanes] for p in range(HALO)
             ]
@@ -437,7 +472,7 @@
                 tend[c, x, where, lanes] = tend[c, x, where, lanes] + total
             return inner
 
-        lax.fori_loop(0, rows // 8 * PARTS, tile, 0)
+        lax.fori_loop(0, rows // 8 * (span // TILE), tile, 0)
         return carry
 
     lax.fori_loop(0, 3, stream_step, 0)
@@ -446,10 +481,7 @@
         c, lanes = place(t)
         for d in range(1, group):
             ret(t, d).wait_recv()
-        tendency = tend[c, :, :, lanes] + ret_in[c, :, :, lanes]
-        following = keep_rate * acc[c, :, :, lanes] + step_size * tendency
-        acc_out[c, :, :, lanes] = following
-        vel_out[c, :, :, lanes] = vel[c, :, :, lanes] + update_rate * following
+        tend[c, :, :, lanes] = tend[c, :, :, lanes] + ret_in[c, :, :, lanes]
         return carry
 
     lax.fori_loop(0, chunks, last_step, 0)
@@ -459,7 +491,7 @@
             fwd(t, d).wait_send()
             ret(t, d).wait_send()
 
-        @pl.when(source)
+        @pl.when(jnp.logical_and(last, me == shift(t)))
         def _():
             for k in range(group):
                 inf(t, k).wait_send()
@@ -493,23 +525,25 @@
     height = rows * group
     chunks = 3 * PARTS
     even, odd = folded_tables(span)
-    wall = jnp.concatenate([wall_first, wall_second], 0)
-    mix = interpolation(recycle_rows, weight_index, weight_table, height)
     whole = pl.BlockSpec(memory_space=pltpu.VMEM)
     shape = jax.ShapeDtypeStruct(velocity.shape, jnp.float32)
     dma = pltpu.SemaphoreType.DMA
     slab = pltpu.VMEM((3, planes, rows, span), jnp.float32)
     exchanged = pltpu.VMEM((3, group, rows, span), jnp.float32)
     halo = pltpu.VMEM((3, HALO, rows, span), jnp.float32)
-    return pl.pallas_call(
+    tendency = pl.pallas_call(
         functools.partial(section_kernel, slabs, group),
-        out_shape=(shape, shape),
-        in_specs=[whole] * 6,
-        out_specs=(whole, whole),
+        out_shape=shape,
+        in_specs=[pl.BlockSpec(memory_space=pl.ANY)] * 5 + [whole] * 3,
+        out_specs=whole,
         scratch_shapes=[
+            slab,
+            pltpu.VMEM((2 * height, height), jnp.float32),
+            pltpu.VMEM(even.shape, jnp.float32),
+            pltpu.VMEM(odd.shape, jnp.float32),
+            pltpu.VMEM((height, height), jnp.float32),
             exchanged,
             exchanged,
-            slab,
             slab,
             halo,
             halo,
@@ -524,11 +558,23 @@
             dma((3,)),
             dma((chunks, group)),
             dma((chunks,)),
+            dma((7,)),
         ],
         compiler_params=pltpu.CompilerParams(
             collective_id=0, has_side_effects=True, vmem_limit_bytes=60 * 1024 * 1024
         ),
-    )(velocity, accumulated, wall, mix, jnp.asarray(even), jnp.asarray(odd))
+    )(
+        velocity,
+        wall_first,
+        wall_second,
+        jnp.asarray(even),
+        jnp.asarray(odd),
+        recycle_rows.reshape(1, -1),
+        weight_index.reshape(1, -1),
+        weight_table.reshape(1, -1),
+    )
+    accumulated_next = keep_rate * accumulated + step_size * tendency
+    return (velocity + update_rate * accumulated_next, accumulated_next)
 
 
 def solution(mesh):

time: 195 us -> 185 us (0.949)
  the two profiles are of different devices: /device:TPU:30 before, /device:TPU:0 now
where the time goes in v2:
time: 185 us
  Pallas kernels  175 us (95%)
  other arithmetic  7.18 us (4%)
  local copies, waits for them, and re-layouts  2.49 us (1%)
    pallas_call x1, Pallas kernels, fast_shards(): pl.pallas_call(functools.partial(section_kernel, slabs, group), out_shape...  175 us
    add x1, other arithmetic, fast_shards(): return (velocity + update_rate * accumulated_next, accumulated_next)  7.18 us

profile of v2, /device:TPU:0, one launch (start us, length us, event | category | flops | bytes accessed | tf_op | source)
XLA Modules:
  0.0 185.0 jit_solution(6931518284421993119)
XLA Ops:
  0.6 1.2 reshape.13.entries
  1.9 1.2 reshape.14.picks
  3.1 0.0 copy-start
  3.1 174.7 %shard_map.104 = f32[3,4,96,768]{3,2,1,0:T(8,128)} custom-call(f32[3,4,96,768]{3,2,1,0:T(8,128)} %vel_hbm.1, f32[384,384]{1,0:T(8,128)} %first_hbm.1, f32[384,384]{1,0:T(8,128)} %second_hbm.1, f32[384,768]{1,0:T(8,128)} %constant.10.clone.even_hbm, f32[384,768]{1,0:T(8,128)} %constant.11.clone.odd_hbm, s32[1,384]{1,0:T(1,128)} %reshape.13.entries, ...), custom_call_target="tpu_custom_call" | custom-call | tf_op jit(solution)/shard_map/pallas_call | solution.py:534
  177.8 0.0 copy-done
  177.8 7.2 %multiply_add_fusion = (f32[3,4,96,768]{3,2,1,0:T(8,128)}, f32[3,4,96,768]{3,2,1,0:T(8,128)}) fusion(f32[3,4,96,768]{3,2,1,0:T(8,128)S(1)} %copy-done, f32[3,4,96,768]{3,2,1,0:T(8,128)} %shard_map.104, f32[3,4,96,768]{3,2,1,0:T(8,128)} %param.10), kind=kLoop, calls=%fused_computation | loop fusion | flops 4423680 | bytes 17694720 | tf_op jit(solution)/shard_map/add | solution.py:577
Async XLA Ops:
  3.1 174.7 %copy-start = (f32[3,4,96,768]{3,2,1,0:T(8,128)S(1)}, f32[3,4,96,768]{3,2,1,0:T(8,128)}, u32[]{:S(2)}) copy-start(f32[3,4,96,768]{3,2,1,0:T(8,128)} %vel_hbm.1) | copy-start | bytes 10616836

commit v3 on v2

--- a/solution.py
+++ b/solution.py
@@ -359,9 +359,27 @@
     )
     pl.semaphore_wait(barrier, expected)
 
+    def mixes(t, device):
+        return jnp.logical_and(last, device == shift(t))
+
+    def send_recycle(t, carry):
+        for d in range(1, group):
+
+            @pl.when(mixes(t, lax.rem(me + d, group)))
+            def _():
+                fwd(t, d).start()
+
+        return carry
+
+    lax.fori_loop(0, chunks, send_recycle, 0)
+
     def send_fwd(t, carry):
         for d in range(1, group):
-            fwd(t, d).start()
+
+            @pl.when(jnp.logical_not(mixes(t, lax.rem(me + d, group))))
+            def _():
+                fwd(t, d).start()
+
         return carry
 
     lax.fori_loop(0, PARTS, send_fwd, 0)
@@ -383,9 +401,10 @@
     @pl.when(source)
     def _():
         levels = lax.broadcasted_iota(jnp.int32, (table.shape[1], height), 0)
-        chosen = jnp.where(levels == picks[...], 1.0, 0.0)
+        chosen = jnp.where(levels == picks[...].reshape(1, height), 1.0, 0.0)
         frac = exact_dot(jnp.broadcast_to(table[...], (8, table.shape[1])), chosen)[:1]
-        apart = lax.broadcasted_iota(jnp.int32, (height, height), 0) - entries[...]
+        apart = lax.broadcasted_iota(jnp.int32, (height, height), 0)
+        apart = apart - entries[...].reshape(1, height)
         upright = jnp.where(apart == 0, 1.0 - frac, jnp.where(apart == 1, frac, 0.0))
         mix[...] = upright.T
 
@@ -393,6 +412,23 @@
     def _():
         for c in range(3):
             hi[c, 0] = vel[c, planes - 1]
+
+    def inflow_step(t, carry):
+        @pl.when(mixes(t, me))
+        def _():
+            c, lanes = place(t)
+            for d in range(1, group):
+                fwd(t, d).wait_recv()
+            gath[c, me, :, lanes] = vel[c, plane_of(me, t), :, lanes]
+            columns = gath[c, :, :, lanes].reshape(height, width)
+            mixed = exact_dot(mix[...], columns)
+            inf_src[c, :, :, lanes] = mixed.reshape(group, rows, width)
+            for k in range(group):
+                inf(t, k).start()
+
+        return carry
+
+    lax.fori_loop(0, chunks, inflow_step, 0)
 
     def spanwise_step(c, carry):
         left = vel[c, :, :, :half].reshape(planes * rows, half)
@@ -411,8 +447,11 @@
 
     def wall_step(t, carry):
         c, lanes = place(t)
-        for d in range(1, group):
-            fwd(t, d).wait_recv()
+        @pl.when(jnp.logical_not(mixes(t, me)))
+        def _():
+            for d in range(1, group):
+                fwd(t, d).wait_recv()
+
         gath[c, me, :, lanes] = vel[c, plane_of(me, t), :, lanes]
         columns = gath[c, :, :, lanes].reshape(height, width)
         normal = gath[1, :, :, lanes].reshape(height, width)
@@ -422,13 +461,6 @@
         for d in range(1, group):
             ret(t, d).start()
         ret_in[c, plane_of(me, t), :, lanes] = ret_src[c, me, :, lanes]
-
-        @pl.when(jnp.logical_and(last, me == shift(t)))
-        def _():
-            mixed = exact_dot(mix[...], columns)
-            inf_src[c, :, :, lanes] = mixed.reshape(group, rows, width)
-            for k in range(group):
-                inf(t, k).start()
 
         return carry
 
@@ -569,8 +601,8 @@
         wall_second,
         jnp.asarray(even),
         jnp.asarray(odd),
-        recycle_rows.reshape(1, -1),
-        weight_index.reshape(1, -1),
+        recycle_rows,
+        weight_index,
         weight_table.reshape(1, -1),
     )
     accumulated_next = keep_rate * accumulated + step_size * tendency

time: 185 us -> 177 us (0.957)
  the two profiles are of different devices: /device:TPU:0 before, /device:TPU:15 now
where the time goes in v3:
time: 177 us
  Pallas kernels  169 us (95%)
  other arithmetic  7.18 us (4%)
    pallas_call x1, Pallas kernels, fast_shards(): pl.pallas_call(functools.partial(section_kernel, slabs, group), out_shape...  169 us
    add x1, other arithmetic, fast_shards(): return (velocity + update_rate * accumulated_next, accumulated_next)  7.18 us

profile of v3, /device:TPU:15, one launch (start us, length us, event | category | flops | bytes accessed | tf_op | source)
XLA Modules:
  0.0 177.3 jit_solution(13214899392823132563)
XLA Ops:
  0.6 0.0 copy-start
  0.6 169.4 %shard_map.104 = f32[3,4,96,768]{3,2,1,0:T(8,128)} custom-call(f32[3,4,96,768]{3,2,1,0:T(8,128)} %vel_hbm.1, f32[384,384]{1,0:T(8,128)} %first_hbm.1, f32[384,384]{1,0:T(8,128)} %second_hbm.1, f32[384,768]{1,0:T(8,128)} %constant.10.clone.even_hbm, f32[384,768]{1,0:T(8,128)} %constant.11.clone.odd_hbm, s32[384]{0:T(512)} %entries.1, s32[384]{0:T(512)} %picks.1, ...), custom_call_target="tpu_custom_call" | custom-call | tf_op jit(solution)/shard_map/pallas_call | solution.py:566
  170.1 0.0 copy-done
  170.1 7.2 %multiply_add_fusion = (f32[3,4,96,768]{3,2,1,0:T(8,128)}, f32[3,4,96,768]{3,2,1,0:T(8,128)}) fusion(f32[3,4,96,768]{3,2,1,0:T(8,128)S(1)} %copy-done, f32[3,4,96,768]{3,2,1,0:T(8,128)} %shard_map.104, f32[3,4,96,768]{3,2,1,0:T(8,128)} %param.10), kind=kLoop, calls=%fused_computation | loop fusion | flops 4423680 | bytes 17694720 | tf_op jit(solution)/shard_map/add | solution.py:609
Async XLA Ops:
  0.6 169.5 %copy-start = (f32[3,4,96,768]{3,2,1,0:T(8,128)S(1)}, f32[3,4,96,768]{3,2,1,0:T(8,128)}, u32[]{:S(2)}) copy-start(f32[3,4,96,768]{3,2,1,0:T(8,128)} %vel_hbm.1) | copy-start | bytes 10616836

commit v4 on v3

--- a/solution.py
+++ b/solution.py
@@ -232,6 +232,9 @@
     inf_send,
     inf_recv,
     load_sem,
+    relay,
+    relay_send,
+    relay_recv,
 ):
     gx = lax.axis_index("gx")
     me = lax.axis_index("ga")
@@ -244,6 +247,9 @@
     not_last = gx < slabs - 1
     last = gx == slabs - 1
     source = jnp.logical_and(last, jnp.logical_and(me >= 1, me <= SHIFTS))
+    inner = jnp.logical_and(me >= 1, me <= SHIFTS)
+    middle_relay = jnp.logical_and(gx == 2, inner)
+    inlet_relay = jnp.logical_and(gx == 0, inner)
     loads = [pltpu.make_async_copy(vel_hbm.at[c], vel.at[c], load_sem.at[c]) for c in range(3)]
     loads += [
         pltpu.make_async_copy(even_hbm, even, load_sem.at[3]),
@@ -301,6 +307,36 @@
             device_id_type=MESH,
         )
 
+    def to_relay(turn):
+        t = turn * PARTS + me - 1
+        c, lanes = place(t)
+        return pltpu.make_async_remote_copy(
+            src_ref=inf_src.at[c, :, :, lanes],
+            dst_ref=relay,
+            send_sem=inf_send.at[t, 0],
+            recv_sem=relay_recv.at[0],
+            device_id={"gx": 2 * turn},
+            device_id_type=MESH,
+        )
+
+    def from_relay(turn, k):
+        t = turn * PARTS + me - 1
+        c, lanes = place(t)
+        return pltpu.make_async_remote_copy(
+            src_ref=relay.at[k],
+            dst_ref=lo.at[c, 0, :, lanes],
+            send_sem=relay_send.at[k],
+            recv_sem=inf_recv.at[t],
+            device_id={"gx": 0, "ga": k},
+            device_id_type=MESH,
+        )
+
+    def own_relay():
+        c, lanes = place(me - 1)
+        return pltpu.make_async_copy(
+            relay.at[me], lo.at[c, 0, :, lanes], inf_recv.at[me - 1]
+        )
+
     def upward(c):
         return pltpu.make_async_remote_copy(
             src_ref=vel_hbm.at[c],
@@ -349,13 +385,33 @@
                 barrier, inc=1, device_id={"gx": 0, "ga": k}, device_id_type=MESH
             )
 
+    @pl.when(gx == 0)
+    def _():
+        for k in range(1, SHIFTS + 1):
+            pl.semaphore_signal(
+                barrier, inc=1, device_id={"gx": 2, "ga": k}, device_id_type=MESH
+            )
+
+    @pl.when(source)
+    def _():
+        pl.semaphore_signal(barrier, inc=1, device_id={"gx": 2}, device_id_type=MESH)
+
+    @pl.when(middle_relay)
+    def _():
+        pl.semaphore_signal(barrier, inc=1, device_id={"gx": slabs - 1}, device_id_type=MESH)
+        for k in range(group):
+            pl.semaphore_signal(
+                barrier, inc=1, device_id={"gx": 0, "ga": k}, device_id_type=MESH
+            )
+
     expected = (
         group
         - 1
         + not_first.astype(jnp.int32)
         + not_last.astype(jnp.int32)
-        + SHIFTS * (gx == 0).astype(jnp.int32)
-        + group * source.astype(jnp.int32)
+        + 2 * SHIFTS * (gx == 0).astype(jnp.int32)
+        + (group + 1) * source.astype(jnp.int32)
+        + (group + 1) * middle_relay.astype(jnp.int32)
     )
     pl.semaphore_wait(barrier, expected)
 
@@ -423,8 +479,16 @@
             columns = gath[c, :, :, lanes].reshape(height, width)
             mixed = exact_dot(mix[...], columns)
             inf_src[c, :, :, lanes] = mixed.reshape(group, rows, width)
-            for k in range(group):
-                inf(t, k).start()
+            for turn in range(2):
+
+                @pl.when(t // PARTS == turn)
+                def _():
+                    to_relay(turn).start()
+
+            @pl.when(t // PARTS == 2)
+            def _():
+                for k in range(group):
+                    inf(t, k).start()
 
         return carry
 
@@ -444,6 +508,19 @@
         return carry
 
     lax.fori_loop(0, 3, spanwise_step, 0)
+
+    @pl.when(inlet_relay)
+    def _():
+        to_relay(0).wait_recv()
+        own_relay().start()
+        for d in range(1, group):
+            from_relay(0, lax.rem(me + d, group)).start()
+
+    @pl.when(middle_relay)
+    def _():
+        to_relay(1).wait_recv()
+        for k in range(group):
+            from_relay(1, k).start()
 
     def wall_step(t, carry):
         c, lanes = place(t)
@@ -525,12 +602,31 @@
 
         @pl.when(jnp.logical_and(last, me == shift(t)))
         def _():
-            for k in range(group):
-                inf(t, k).wait_send()
+            for turn in range(2):
+
+                @pl.when(t // PARTS == turn)
+                def _():
+                    to_relay(turn).wait_send()
+
+            @pl.when(t // PARTS == 2)
+            def _():
+                for k in range(group):
+                    inf(t, k).wait_send()
 
         return carry
 
     lax.fori_loop(0, chunks, drain, 0)
+
+    @pl.when(inlet_relay)
+    def _():
+        for d in range(1, group):
+            from_relay(0, lax.rem(me + d, group)).wait_send()
+
+    @pl.when(middle_relay)
+    def _():
+        for k in range(group):
+            from_relay(1, k).wait_send()
+
     for c in range(3):
 
         @pl.when(not_last)
@@ -591,6 +687,9 @@
             dma((chunks, group)),
             dma((chunks,)),
             dma((7,)),
+            pltpu.VMEM((group, rows, span // PARTS), jnp.float32),
+            dma((group,)),
+            dma((1,)),
         ],
         compiler_params=pltpu.CompilerParams(
             collective_id=0, has_side_effects=True, vmem_limit_bytes=60 * 1024 * 1024
@@ -616,7 +715,7 @@
 
     def body(velocity, *others):
         _, planes, rows, span = velocity.shape
-        if planes == HALO == group and slabs > 2 and rows % 8 == 0 and span % 768 == 0:
+        if planes == HALO == group and slabs > 3 and rows % 8 == 0 and span % 768 == 0:
             return fast_shards(slabs, group, velocity, *others)
         return shards(velocity, *others)
 

time: 177 us -> 172 us (0.972)
  the two profiles are of different devices: /device:TPU:15 before, /device:TPU:0 now
where the time goes in v4:
time: 172 us
  Pallas kernels  164 us (95%)
  other arithmetic  7.18 us (4%)
    pallas_call x1, Pallas kernels, fast_shards(): pl.pallas_call(functools.partial(section_kernel, slabs, group), out_shape...  164 us
    add x1, other arithmetic, fast_shards(): return (velocity + update_rate * accumulated_next, accumulated_next)  7.18 us

profile of v4, /device:TPU:0, one launch (start us, length us, event | category | flops | bytes accessed | tf_op | source)
XLA Modules:
  0.0 171.9 jit_solution(13965700033779876196)
XLA Ops:
  0.6 0.0 copy-start
  0.6 164.1 %shard_map.104 = f32[3,4,96,768]{3,2,1,0:T(8,128)} custom-call(f32[3,4,96,768]{3,2,1,0:T(8,128)} %vel_hbm.1, f32[384,384]{1,0:T(8,128)} %first_hbm.1, f32[384,384]{1,0:T(8,128)} %second_hbm.1, f32[384,768]{1,0:T(8,128)} %constant.10.clone.even_hbm, f32[384,768]{1,0:T(8,128)} %constant.11.clone.odd_hbm, s32[384]{0:T(512)} %entries.1, s32[384]{0:T(512)} %picks.1, ...), custom_call_target="tpu_custom_call" | custom-call | tf_op jit(solution)/shard_map/pallas_call | solution.py:662
  164.7 0.0 copy-done
  164.7 7.2 %multiply_add_fusion = (f32[3,4,96,768]{3,2,1,0:T(8,128)}, f32[3,4,96,768]{3,2,1,0:T(8,128)}) fusion(f32[3,4,96,768]{3,2,1,0:T(8,128)S(1)} %copy-done, f32[3,4,96,768]{3,2,1,0:T(8,128)} %shard_map.104, f32[3,4,96,768]{3,2,1,0:T(8,128)} %param.10), kind=kLoop, calls=%fused_computation | loop fusion | flops 4423680 | bytes 17694720 | tf_op jit(solution)/shard_map/add | solution.py:708
Async XLA Ops:
  0.6 164.1 %copy-start = (f32[3,4,96,768]{3,2,1,0:T(8,128)S(1)}, f32[3,4,96,768]{3,2,1,0:T(8,128)}, u32[]{:S(2)}) copy-start(f32[3,4,96,768]{3,2,1,0:T(8,128)} %vel_hbm.1) | copy-start | bytes 10616836
